TPU v7x, 32 devices: a whole 2x2x4 slice. The times are simulated.
32 devices in a mesh: gx: 8 (over z, y), gy: 4 (over x, core).
Axes of the slice: x: 2, y: 2, z: 4, core: 2. Of those that a mesh axis runs over, the one named last changes fastest.
Arguments:
- modes_start: float32 [16, 64, 2048], P(None, 'gx', 'gy'), may hold values from -6 to 6
- search_start: float32 [16, 64, 2048], P(None, 'gx', 'gy'), may hold values from -6 to 6
- stiffness: float32 [64, 2048], P('gx', 'gy'), may hold values from 1 to 10
- density: float32 [64, 2048], P('gx', 'gy'), may hold values from 0.3 to 3
Outputs:
- modes: float32 [16, 64, 2048], P(None, 'gx', 'gy')
- search: float32 [16, 64, 2048], P(None, 'gx', 'gy')
- ritz: float32 [16], replicated
All inputs are finite; a program needn't handle non-finite values.
Results may differ from a plain program's by a relative error of at most 0.00018.
Values sent between devices are 32-bit elements; how exact they have to be, the bound alone decides.
A program may use at most 64 MiB of HBM per device.

v0:
```python
import math

import jax
import jax.numpy as jnp
from jax import lax
from jax.sharding import PartitionSpec as P

NZ = 16
MODES = 16
ITERS = 2
INNER = 6


SHIFTS = [
    (first, second, third) for first in (-1, 0, 1) for second in (-1, 0, 1) for third in (-1, 0, 1)
]


def swapped(value, axis, distance):
    return lax.ppermute(value, axis, [(i, i ^ 1 << distance) for i in range(lax.axis_size(axis))])


def with_halo(value, sides, width):
    for axis, dim in sides:
        peers, length = (lax.axis_size(axis), value.shape[dim])
        up = [(i, (i + 1) % peers) for i in range(peers - 1)]
        down = [(j, i) for i, j in up]
        last = lax.slice_in_dim(value, length - width, length, axis=dim)
        first = lax.slice_in_dim(value, 0, width, axis=dim)
        before = lax.ppermute(last, axis, up)
        after = lax.ppermute(first, axis, down)
        value = jnp.concatenate([before, value, after], axis=dim)
    return value


def stiff_weight(shift):
    nonzero = sum((1 for value in shift if value != 0))
    return 1.0 / 2 ** (nonzero - 1)


def mass_weight(shift):
    product = 1.0
    for value in shift:
        product = product * (4.0 / 6.0 if value == 0 else 1.0 / 6.0)
    return product


def solve_lower(lower, right):
    return lax.linalg.triangular_solve(lower, right, left_side=True, lower=True)


def solve_upper_t(lower, right):
    return lax.linalg.triangular_solve(lower, right, left_side=True, lower=True, transpose_a=True)


def project(lower, matrix):
    first_half = solve_lower(lower, matrix)
    second_half = solve_lower(lower, first_half.T)
    return 0.5 * (second_half + second_half.T)


def small_problem(lower_gram, stiff_gram, mass_gram):
    proj_stiff = project(lower_gram, stiff_gram)
    proj_mass = project(lower_gram, mass_gram)
    lower_stiff = jnp.linalg.cholesky(proj_stiff)
    block_width = proj_stiff.shape[0]
    columns = jnp.eye(block_width, MODES, dtype=jnp.float32)
    for inner_index in range(INNER):
        moved = jnp.dot(proj_mass, columns, precision=lax.Precision.HIGHEST)
        solved = solve_upper_t(lower_stiff, solve_lower(lower_stiff, moved))
        correlation = jnp.dot(
            solved.T,
            jnp.dot(proj_mass, solved, precision=lax.Precision.HIGHEST),
            precision=lax.Precision.HIGHEST,
        )
        correlation = 0.5 * (correlation + correlation.T)
        lower_correlation = jnp.linalg.cholesky(correlation)
        columns = solve_lower(lower_correlation, solved.T).T
    ritz_values = jnp.sum(
        columns * jnp.dot(proj_stiff, columns, precision=lax.Precision.HIGHEST), axis=0
    )
    trimmed = jnp.concatenate([jnp.zeros((MODES, MODES), jnp.float32), columns[MODES:]], axis=0)
    return (solve_upper_t(lower_gram, columns), solve_upper_t(lower_gram, trimmed), ritz_values)


def flatten_padded(padded):
    merged = padded.reshape(padded.shape[:-2] + (padded.shape[-2] * padded.shape[-1],))
    return jnp.pad(merged, [(0, 0)] * (merged.ndim - 1) + [(1, 1)])


def take_tap(padded_flat, shift, row_count, lane_count):
    first, second, third = shift
    begin_col = 1 + (1 + second) * NZ + third
    return padded_flat[..., 1 + first : 1 + first + row_count, begin_col : begin_col + lane_count]


def depth_masks(lane_count):
    depth_pos = lax.iota(jnp.int32, lane_count) % NZ
    return {
        -1: (depth_pos >= 1).astype(jnp.float32),
        0: jnp.ones((lane_count,), jnp.float32),
        1: (depth_pos <= NZ - 2).astype(jnp.float32),
    }


def apply_operators(field_padded, coeff_flat, stiff_center, root_center):
    width_cols = field_padded.shape[0]
    row_count = field_padded.shape[1] - 2
    lane_count = (field_padded.shape[2] - 2) * NZ
    field_flat = flatten_padded(field_padded)
    masks = depth_masks(lane_count)
    center = take_tap(field_flat, (0, 0, 0), row_count, lane_count)
    scaled_flat = coeff_flat[1] * field_flat
    stiff_out = jnp.zeros_like(center)
    mass_sum = jnp.zeros_like(center)
    for shift in SHIFTS:
        depth_mask = masks[shift[2]]
        if shift != (0, 0, 0):
            neighbour = take_tap(field_flat, shift, row_count, lane_count) * depth_mask
            stiff_near = take_tap(coeff_flat[0], shift, row_count, lane_count) * depth_mask
            stiff_out = stiff_out + stiff_weight(shift) * 0.5 * (stiff_center + stiff_near) * (
                center - neighbour
            )
        mass_sum = (
            mass_sum
            + mass_weight(shift) * take_tap(scaled_flat, shift, row_count, lane_count) * depth_mask
        )
    mass_out = root_center * mass_sum
    return (stiff_out.reshape(width_cols, -1), mass_out.reshape(width_cols, -1))


def as_grid(block_mat, row_count):
    return block_mat.reshape(block_mat.shape[0], row_count, -1, NZ)


def rayleigh_sums(current, stiff_modes, mass_modes):
    numer, denom = lax.psum(
        (jnp.sum(current * stiff_modes, axis=1), jnp.sum(current * mass_modes, axis=1)),
        ("gx", "gy"),
    )
    return stiff_modes - mass_modes * (numer / denom)[:, None]


def reduce_block(wide, stiff_wide, mass_wide):
    gram_local = jnp.dot(wide, wide.T, precision=lax.Precision.HIGHEST)
    stiff_local = jnp.dot(wide, stiff_wide.T, precision=lax.Precision.HIGHEST)
    mass_local = jnp.dot(wide, mass_wide.T, precision=lax.Precision.HIGHEST)
    lower_gram = jnp.linalg.cholesky(gram_local)
    for bit_index in range(lax.axis_size("gx").bit_length() - 1):
        partner = swapped(lower_gram, "gx", bit_index)
        lower_gram = jnp.linalg.cholesky(
            jnp.dot(lower_gram, lower_gram.T, precision=lax.Precision.HIGHEST)
            + jnp.dot(partner, partner.T, precision=lax.Precision.HIGHEST)
        )
    for bit_index in range(lax.axis_size("gy").bit_length() - 1):
        partner = swapped(lower_gram, "gy", bit_index)
        lower_gram = jnp.linalg.cholesky(
            jnp.dot(lower_gram, lower_gram.T, precision=lax.Precision.HIGHEST)
            + jnp.dot(partner, partner.T, precision=lax.Precision.HIGHEST)
        )
    stiff_gram, mass_gram = lax.psum((stiff_local, mass_local), ("gx", "gy"))
    return small_problem(lower_gram, stiff_gram, mass_gram)


def on_device(modes_start, search_start, stiffness, density):
    row_count = stiffness.shape[0]
    lane_count = stiffness.shape[1]
    root_center = jnp.sqrt(density)
    coeff_stack = jnp.stack([stiffness, root_center]).reshape(2, row_count, -1, NZ)
    coeff_padded = with_halo(coeff_stack, (("gx", 1), ("gy", 2)), 1)
    coeff_flat = flatten_padded(coeff_padded)
    current = modes_start.reshape(MODES, -1)
    search = search_start.reshape(MODES, -1)
    ritz_values = jnp.zeros((MODES,), jnp.float32)
    for iteration in range(ITERS):
        mode_padded = with_halo(as_grid(current, row_count), (("gx", 1), ("gy", 2)), 1)
        stiff_modes, mass_modes = apply_operators(mode_padded, coeff_flat, stiffness, root_center)
        residual = rayleigh_sums(current, stiff_modes, mass_modes)
        rest = jnp.concatenate([residual, search], axis=0)
        rest_padded = with_halo(as_grid(rest, row_count), (("gx", 1), ("gy", 2)), 1)
        stiff_rest, mass_rest = apply_operators(rest_padded, coeff_flat, stiffness, root_center)
        wide = jnp.concatenate([current, rest], axis=0)
        stiff_wide = jnp.concatenate([stiff_modes, stiff_rest], axis=0)
        mass_wide = jnp.concatenate([mass_modes, mass_rest], axis=0)
        coef_modes, coef_search, ritz_values = reduce_block(wide, stiff_wide, mass_wide)
        current = jnp.dot(coef_modes.T, wide, precision=lax.Precision.HIGHEST)
        search = jnp.dot(coef_search.T, wide, precision=lax.Precision.HIGHEST)
    total_cells = row_count * lane_count * lax.axis_size("gx") * lax.axis_size("gy")
    scale_factor = math.sqrt(total_cells)
    modes_out = (current * scale_factor).reshape(MODES, row_count, lane_count)
    search_out = (search * scale_factor).reshape(MODES, row_count, lane_count)
    return (modes_out, search_out, ritz_values)


def solution(mesh):
    in_specs = (P(None, "gx", "gy"), P(None, "gx", "gy"), P("gx", "gy"), P("gx", "gy"))
    out_specs = (P(None, "gx", "gy"), P(None, "gx", "gy"), P())
    return jax.shard_map(
        on_device, mesh=mesh, in_specs=in_specs, out_specs=out_specs, check_vma=False
    )
```

profile of v0, /device:TPU:0, one launch (start us, length us, event | category | flops | bytes accessed | tf_op | source)
XLA Modules:
  0.0 540.7 jit_solution(6573713932030442332)
XLA Ops:
  2.4 4.9 collective-permute-start
  11.4 5.2 collective-permute-start.4
  33.0 4.3 collective-permute-start.6
  46.6 5.4 multiply_reduce_fusion.2
  54.5 43.3 %all-reduce.10 = (f32[16]{0:T(128)S(1)}, f32[16]{0:T(128)S(1)}) all-reduce(f32[16]{0:T(128)} %get-tuple-element.12, f32[16]{0:T(128)} %get-tuple-element.10), channel_id=1, replica_groups=mesh['gx'=8,'gy'=4] {'gx','gy'}, use_global_device_ids=true, to_apply=%region_1.2 | all-reduce | flops 32 | bytes 256 | tf_op jit(solution)/shard_map/psum | solution.py:137
  99.7 4.4 cholesky.416
  121.7 4.4 cholesky.427
  127.4 4.5 collective-permute-start.9
  132.1 5.0 collective-permute-done.9
  137.4 4.4 cholesky.438
  148.2 4.4 cholesky.449
  155.4 4.4 cholesky.460
  165.3 4.4 cholesky.471
  176.3 3.7 custom-call.82
  180.0 7.6 %pad_maximum_fusion = f32[32,10,34,16]{3,2,1,0:T(8,128)} fusion(f32[32,10,1,16]{3,2,1,0:T(1,128)} %collective-permute-done.16, f32[32,1,32,16]{3,2,1,0:T(8,128)} %collective-permute-done.14, f32[16,8,32,16]{3,2,1,0:T(8,128)S(1)} %concatenate.71, f32[16,8,32,16]{3,2,1,0:T(8,128)} %copy-done, f32[32,1,32,16]{3,2,1,0:T(8,128)} %collective-permute-done.13, ...), kind=kLoop, calls=%fused_computation | loop fusion | flops 870400 | bytes 1392640 | tf_op jit(solution)/shard_map/concatenate | solution.py:32
  187.6 6.0 %copy.419 = f32[32,10,34,16]{0,3,2,1:T(8,128)} copy(f32[32,10,34,16]{3,2,1,0:T(8,128)} %pad_maximum_fusion) | data formatting | bytes 1392640 | tf_op jit(solution)/shard_map/concatenate | solution.py:32
  197.5 3.7 fusion.54
  207.6 40.0 %all-reduce.9 = (f32[48,48]{1,0:T(8,128)S(1)}, f32[48,48]{1,0:T(8,128)S(1)}) all-reduce(f32[48,48]{1,0:T(8,128)S(1)} %fusion.5, f32[48,48]{1,0:T(8,128)S(1)} %fusion.1), channel_id=1, replica_groups=mesh['gx'=8,'gy'=4] {'gx','gy'}, use_global_device_ids=true, to_apply=%region_7.10 | all-reduce | flops 4608 | bytes 36864 | tf_op jit(solution)/shard_map/psum | solution.py:161
  248.3 4.4 cholesky.482
  290.7 4.2 collective-permute-start.17
  296.3 9.4 %collective-permute-done.17 = f32[16,1,32,16]{3,2,1,0:T(8,128)S(1)} collective-permute-done((f32[16,1,32,16]{3,2,1,0:T(8,128)S(1)}, f32[16,1,32,16]{3,2,1,0:T(8,128)S(1)}, u32[]{:S(2)}, u32[]{:S(2)}) %collective-permute-start.17) | collective-permute-done | bytes 32800 | tf_op jit(solution)/shard_map/ppermute | solution.py:30
  321.0 42.9 %all-reduce.8 = (f32[16]{0:T(128)S(1)}, f32[16]{0:T(128)S(1)}) all-reduce(f32[16]{0:T(128)S(1)} %get-tuple-element.8, f32[16]{0:T(128)S(1)} %get-tuple-element.6), channel_id=1, replica_groups=mesh['gx'=8,'gy'=4] {'gx','gy'}, use_global_device_ids=true, to_apply=%region_11.18 | all-reduce | flops 32 | bytes 256 | tf_op jit(solution)/shard_map/psum | solution.py:137
  368.2 4.4 cholesky.559
  380.8 4.4 cholesky.570
  392.0 4.4 cholesky.581
  402.7 4.4 cholesky.592
  410.0 4.4 cholesky.603
  419.8 4.4 cholesky.614
  430.4 3.7 custom-call.106
  441.0 4.5 fusion.92
  451.6 43.1 %all-reduce.7 = (f32[48,48]{1,0:T(8,128)S(1)}, f32[48,48]{1,0:T(8,128)S(1)}) all-reduce(f32[48,48]{1,0:T(8,128)S(1)} %fusion.13, f32[48,48]{1,0:T(8,128)S(1)} %fusion.9), channel_id=1, replica_groups=mesh['gx'=8,'gy'=4] {'gx','gy'}, use_global_device_ids=true, to_apply=%region_15.22 | all-reduce | flops 4608 | bytes 36864 | tf_op jit(solution)/shard_map/psum | solution.py:161
  495.4 4.4 cholesky.625
  (595 shorter events, 234.4 us)
Async XLA Ops:
  2.4 16.8 %collective-permute-start = (f32[2,1,32,16]{3,2,1,0:T(8,128)S(1)}, f32[2,1,32,16]{3,2,1,0:T(8,128)S(1)}, u32[]{:S(2)}, u32[]{:S(2)}) collective-permute-start(f32[2,1,32,16]{3,2,1,0:T(8,128)S(1)} %get-tuple-element.41), channel_id=1, source_target_pairs={{0,4},{4,8},{8,12},{12,16},{16,20},{20,24},{24,28},{1,5},{5,9},{9,... | collective-permute-start | bytes 12296 | tf_op jit(solution)/shard_map/ppermute | solution.py:30
  7.3 11.9 %collective-permute-start.1 = (f32[2,1,32,16]{3,2,1,0:T(8,128)S(1)}, f32[2,1,32,16]{3,2,1,0:T(8,128)S(1)}, u32[]{:S(2)}, u32[]{:S(2)}) collective-permute-start(f32[2,1,32,16]{3,2,1,0:T(8,128)S(1)} %get-tuple-element.42), channel_id=1, source_target_pairs={{4,0},{8,4},{12,8},{16,12},{20,16},{24,20},{28,24},{5,1},{9,5},{13... | collective-permute-start | bytes 12296 | tf_op jit(solution)/shard_map/ppermute | solution.py:31
  11.4 17.8 %collective-permute-start.4 = (f32[16,1,32,16]{3,2,1,0:T(8,128)}, f32[16,1,32,16]{3,2,1,0:T(8,128)}, u32[]{:S(2)}, u32[]{:S(2)}) collective-permute-start(f32[16,1,32,16]{3,2,1,0:T(8,128)} %get-tuple-element.38), channel_id=1, source_target_pairs={{0,4},{4,8},{8,12},{12,16},{16,20},{20,24},{24,28},{1,5},{5,9},{9,... | collective-permute-start | bytes 98312 | tf_op jit(solution)/shard_map/ppermute | solution.py:30
  16.7 15.3 %collective-permute-start.5 = (f32[16,1,32,16]{3,2,1,0:T(8,128)}, f32[16,1,32,16]{3,2,1,0:T(8,128)}, u32[]{:S(2)}, u32[]{:S(2)}) collective-permute-start(f32[16,1,32,16]{3,2,1,0:T(8,128)} %get-tuple-element.37), channel_id=1, source_target_pairs={{4,0},{8,4},{12,8},{16,12},{20,16},{24,20},{28,24},{5,1},{9,5},{13... | collective-permute-start | bytes 98312 | tf_op jit(solution)/shard_map/ppermute | solution.py:31
  19.2 4.3 collective-permute-start.2
  20.5 4.9 collective-permute-start.3
  23.5 183.3 %copy-start.4 = (f32[2,8,8,512]{3,1,2,0:T(8,128)}, f32[2,8,8,512]{3,1,2,0:T(8,128)S(1)}, u32[]{:S(2)}) copy-start(f32[2,8,8,512]{3,1,2,0:T(8,128)S(1)} %copy.544) | copy-start | bytes 786436
  33.0 7.0 %collective-permute-start.6 = (f32[16,10,1,16]{3,2,1,0:T(1,128)S(1)}, f32[16,10,1,16]{3,2,1,0:T(1,128)S(1)}, u32[]{:S(2)}, u32[]{:S(2)}) collective-permute-start(f32[16,10,1,16]{3,2,1,0:T(1,128)S(1)} %get-tuple-element.31), channel_id=1, source_target_pairs={{0,1},{1,2},{2,3},{4,5},{5,6},{6,7},{8,9},{9,10},{10,11},{12,13},{... | collective-permute-start | bytes 30728 | tf_op jit(solution)/shard_map/ppermute | solution.py:30
  37.4 3.2 collective-permute-start.7
  105.4 16.0 %collective-permute-start.8 = (f32[48,48]{1,0:T(8,128)S(1)}, f32[48,48]{1,0:T(8,128)S(1)}, u32[]{:S(2)}, u32[]{:S(2)}) collective-permute-start(f32[48,48]{1,0:T(8,128)S(1)} %fusion.517), channel_id=1, source_target_pairs={{0,4},{4,0},{8,12},{12,8},{16,20},{20,16},{24,28},{28,24},{1,5},{5... | collective-permute-start | bytes 27656 | tf_op jit(solution)/shard_map/ppermute | solution.py:20
  117.4 52.9 %collective-permute-start.13 = (f32[32,1,32,16]{3,2,1,0:T(8,128)}, f32[32,1,32,16]{3,2,1,0:T(8,128)}, u32[]{:S(2)}, u32[]{:S(2)}) collective-permute-start(f32[32,1,32,16]{3,2,1,0:T(8,128)} %get-tuple-element.25), channel_id=1, source_target_pairs={{0,4},{4,8},{8,12},{12,16},{16,20},{20,24},{24,28},{1,5},{5,9},{9,... | collective-permute-start | bytes 196616 | tf_op jit(solution)/shard_map/ppermute | solution.py:30
  120.1 50.2 %collective-permute-start.14 = (f32[32,1,32,16]{3,2,1,0:T(8,128)}, f32[32,1,32,16]{3,2,1,0:T(8,128)}, u32[]{:S(2)}, u32[]{:S(2)}) collective-permute-start(f32[32,1,32,16]{3,2,1,0:T(8,128)} %get-tuple-element.26), channel_id=1, source_target_pairs={{4,0},{8,4},{12,8},{16,12},{20,16},{24,20},{28,24},{5,1},{9,5},{13... | collective-permute-start | bytes 196616 | tf_op jit(solution)/shard_map/ppermute | solution.py:31
  127.4 9.7 %collective-permute-start.9 = (f32[48,48]{1,0:T(8,128)S(1)}, f32[48,48]{1,0:T(8,128)S(1)}, u32[]{:S(2)}, u32[]{:S(2)}) collective-permute-start(f32[48,48]{1,0:T(8,128)S(1)} %fusion.518), channel_id=1, source_target_pairs={{0,8},{4,12},{8,0},{12,4},{16,24},{20,28},{24,16},{28,20},{1,9},{5... | collective-permute-start | bytes 27656 | tf_op jit(solution)/shard_map/ppermute | solution.py:20
  143.1 4.8 collective-permute-start.10
  153.9 1.3 collective-permute-start.11
  161.1 3.9 collective-permute-start.12
  172.1 7.8 %collective-permute-start.15 = (f32[32,10,1,16]{3,2,1,0:T(1,128)S(1)}, f32[32,10,1,16]{3,2,1,0:T(1,128)}, u32[]{:S(2)}, u32[]{:S(2)}) collective-permute-start(f32[32,10,1,16]{3,2,1,0:T(1,128)S(1)} %get-tuple-element.23), channel_id=1, source_target_pairs={{0,1},{1,2},{2,3},{4,5},{5,6},{6,7},{8,9},{9,10},{10,11},{12,13},{... | collective-permute-start | bytes 61448 | tf_op jit(solution)/shard_map/ppermute | solution.py:30
  174.1 5.9 %collective-permute-start.16 = (f32[32,10,1,16]{3,2,1,0:T(1,128)S(1)}, f32[32,10,1,16]{3,2,1,0:T(1,128)}, u32[]{:S(2)}, u32[]{:S(2)}) collective-permute-start(f32[32,10,1,16]{3,2,1,0:T(1,128)S(1)} %get-tuple-element.24), channel_id=1, source_target_pairs={{1,0},{2,1},{3,2},{5,4},{6,5},{7,6},{9,8},{10,9},{11,10},{13,12},{... | collective-permute-start | bytes 61448 | tf_op jit(solution)/shard_map/ppermute | solution.py:31
  207.6 81.8 %copy-start.5 = (f32[2,8,8,512]{3,1,2,0:T(8,128)S(1)}, f32[2,8,8,512]{3,1,2,0:T(8,128)}, u32[]{:S(2)}) copy-start(f32[2,8,8,512]{3,1,2,0:T(8,128)} %copy-done.4) | copy-start | bytes 786436
  290.7 15.0 %collective-permute-start.17 = (f32[16,1,32,16]{3,2,1,0:T(8,128)S(1)}, f32[16,1,32,16]{3,2,1,0:T(8,128)S(1)}, u32[]{:S(2)}, u32[]{:S(2)}) collective-permute-start(f32[16,1,32,16]{3,2,1,0:T(8,128)S(1)} %get-tuple-element.36), channel_id=1, source_target_pairs={{0,4},{4,8},{8,12},{12,16},{16,20},{20,24},{24,28},{1,5},{5,9},{9,... | collective-permute-start | bytes 98312 | tf_op jit(solution)/shard_map/ppermute | solution.py:30
  294.9 11.1 %collective-permute-start.18 = (f32[16,1,32,16]{3,2,1,0:T(8,128)S(1)}, f32[16,1,32,16]{3,2,1,0:T(8,128)S(1)}, u32[]{:S(2)}, u32[]{:S(2)}) collective-permute-start(f32[16,1,32,16]{3,2,1,0:T(8,128)S(1)} %get-tuple-element.35), channel_id=1, source_target_pairs={{4,0},{8,4},{12,8},{16,12},{20,16},{24,20},{28,24},{5,1},{9,5},{13... | collective-permute-start | bytes 98312 | tf_op jit(solution)/shard_map/ppermute | solution.py:31
  306.1 4.0 collective-permute-start.19
  307.4 4.0 collective-permute-start.20
  373.9 6.7 %collective-permute-start.21 = (f32[48,48]{1,0:T(8,128)S(1)}, f32[48,48]{1,0:T(8,128)S(1)}, u32[]{:S(2)}, u32[]{:S(2)}) collective-permute-start(f32[48,48]{1,0:T(8,128)S(1)} %fusion.522), channel_id=1, source_target_pairs={{0,4},{4,0},{8,12},{12,8},{16,20},{20,16},{24,28},{28,24},{1,5},{5... | collective-permute-start | bytes 27656 | tf_op jit(solution)/shard_map/ppermute | solution.py:20
  376.4 48.5 %collective-permute-start.26 = (f32[32,1,32,16]{0,3,2,1:T(8,128)}, f32[32,1,32,16]{0,3,2,1:T(8,128)}, u32[]{:S(2)}, u32[]{:S(2)}) collective-permute-start(f32[32,1,32,16]{0,3,2,1:T(8,128)} %get-tuple-element.33), channel_id=1, source_target_pairs={{0,4},{4,8},{8,12},{12,16},{16,20},{20,24},{24,28},{1,5},{5,9},{9,... | collective-permute-start | bytes 196616 | tf_op jit(solution)/shard_map/ppermute | solution.py:30
  379.0 45.9 %collective-permute-start.27 = (f32[32,1,32,16]{0,3,2,1:T(8,128)}, f32[32,1,32,16]{0,3,2,1:T(8,128)}, u32[]{:S(2)}, u32[]{:S(2)}) collective-permute-start(f32[32,1,32,16]{0,3,2,1:T(8,128)} %get-tuple-element.34), channel_id=1, source_target_pairs={{4,0},{8,4},{12,8},{16,12},{20,16},{24,20},{28,24},{5,1},{9,5},{13... | collective-permute-start | bytes 196616 | tf_op jit(solution)/shard_map/ppermute | solution.py:31
  386.5 5.2 collective-permute-start.22
  397.7 4.8 collective-permute-start.23
  408.5 1.3 collective-permute-start.24
  415.7 3.9 collective-permute-start.25
  426.3 7.8 %collective-permute-start.28 = (f32[32,10,1,16]{0,3,2,1:T(8,128)}, f32[32,10,1,16]{0,3,2,1:T(8,128)}, u32[]{:S(2)}, u32[]{:S(2)}) collective-permute-start(f32[32,10,1,16]{0,3,2,1:T(8,128)} %get-tuple-element.27), channel_id=1, source_target_pairs={{0,1},{1,2},{2,3},{4,5},{5,6},{6,7},{8,9},{9,10},{10,11},{12,13},{... | collective-permute-start | bytes 61448 | tf_op jit(solution)/shard_map/ppermute | solution.py:30
  428.2 5.9 %collective-permute-start.29 = (f32[32,10,1,16]{0,3,2,1:T(8,128)}, f32[32,10,1,16]{0,3,2,1:T(8,128)}, u32[]{:S(2)}, u32[]{:S(2)}) collective-permute-start(f32[32,10,1,16]{0,3,2,1:T(8,128)} %get-tuple-element.28), channel_id=1, source_target_pairs={{1,0},{2,1},{3,2},{5,4},{6,5},{7,6},{9,8},{10,9},{11,10},{13,12},{... | collective-permute-start | bytes 61448 | tf_op jit(solution)/shard_map/ppermute | solution.py:31
  (78 other events, 364.1 us)
where the time goes:
time: 549 us; the launch traced here: 541 us
  other arithmetic  198 us (36%)
  blocking collectives  169 us (31%)
  starting transfers between devices  63.8 us (12%)
  local copies, waits for them, and re-layouts  48.4 us (9%)
  waiting for transfers between devices  31.8 us (6%)
  matrix products  25.3 us (5%)
    psum x2, blocking collectives, rayleigh_sums(): lax.psum((jnp.sum(current * stiff_modes, axis=1), jnp.sum(current * mass_...  86.2 us
    psum x2, blocking collectives, reduce_block(): stiff_gram, mass_gram = lax.psum((stiff_local, mass_local), ('gx', 'gy'))  83.1 us
    another operation x30, other arithmetic, reduce_block(): jnp.linalg.cholesky(jnp.dot(lower_gram, lower_gram.T, precision=lax.Preci...  50.5 us
    ppermute x10, starting transfers between devices, with_halo(): before = lax.ppermute(last, axis, up)  30.4 us
    another operation x36, other arithmetic, small_problem(): lower_correlation = jnp.linalg.cholesky(correlation)  25.8 us
    another operation x24, other arithmetic, solve_lower(): return lax.linalg.triangular_solve(lower, right, left_side=True, lower=True)  22.5 us
    ppermute x10, starting transfers between devices, swapped(): lax.ppermute(value, axis, [(i, i ^ 1 << distance) for i in range(lax.axis...  19.4 us
    ppermute x10, waiting for transfers between devices, swapped(): lax.ppermute(value, axis, [(i, i ^ 1 << distance) for i in range(lax.axis...  18.6 us
  transfers between devices with their start and end apart: 30, of which 12 were waited for; matrix products, arithmetic and copies ran while one was open for 17% of the time, Pallas kernels for 0%

commit v1 on v0

v1 whole, which is shorter than its diff:
```python
import functools
import math

import jax
import jax.numpy as jnp
from jax import lax
from jax.experimental import pallas as pl
from jax.experimental.pallas import tpu as pltpu
from jax.sharding import PartitionSpec as P

NZ = 16
MODES = 16
POWERS = (2, 2, 1, 1)
MESH = pl.DeviceIdType.MESH
F32 = jnp.float32
HIGHEST = lax.Precision.HIGHEST
WIDE = 3 * MODES
COEF, XLO, PLO, RLO, R2LO, TOP = 0, 8, 24, 40, 56, 72


def dot_nt(left, right):
    return lax.dot_general(left, right, (((1,), (1,)), ((), ())), precision=HIGHEST,
                           preferred_element_type=F32)


def dot_nn(left, right):
    return lax.dot_general(left, right, (((1,), (0,)), ((), ())), precision=HIGHEST,
                           preferred_element_type=F32)


def iota(shape, dim):
    return lax.broadcasted_iota(jnp.int32, shape, dim)


def jordan_step(table, k):
    rows = table.shape[0]
    pivot_row = table[k:k + 1, :] * (1.0 / table[k:k + 1, k:k + 1])
    return jnp.where(iota((rows, 1), 0) == k, pivot_row, table - table[:, k:k + 1] * pivot_row)


def orthonormal(gram, rows_t):
    count = gram.shape[0]
    row_id = iota((count, 1), 0)
    for k in range(count - 1):
        factor = jnp.where(row_id > k, gram[:, k:k + 1] * (1.0 / gram[k:k + 1, k:k + 1]), 0.0)
        gram, rows_t = gram - factor * gram[k:k + 1, :], rows_t - factor * rows_t[k:k + 1, :]
    diag = jnp.sum(jnp.where(iota(gram.shape, 0) == iota(gram.shape, 1), gram, 0.0),
                   axis=1, keepdims=True)
    return rows_t * lax.rsqrt(diag)


def small_problem(table):
    stiff = table[:, 0:WIDE]
    mass = table[:, WIDE:2 * WIDE]
    cross = table[:, 2 * WIDE:2 * WIDE + MODES]
    solved = table
    corner = jnp.concatenate(
        [cross[0:MODES], (iota((MODES, MODES), 0) == iota((MODES, MODES), 1)).astype(F32)], axis=1)
    for k in range(WIDE):
        solved = jordan_step(solved, k)
        if k < MODES:
            corner = jordan_step(corner, k)
    step = solved[:, WIDE:2 * WIDE]
    coef_t = (iota((MODES, WIDE), 0) == iota((MODES, WIDE), 1)).astype(F32)
    for power in POWERS:
        for _ in range(power):
            coef_t = dot_nt(coef_t, step)
        coef_t = orthonormal(dot_nt(dot_nn(coef_t, mass), coef_t), coef_t)
    ritz = jnp.sum(dot_nn(coef_t, stiff) * coef_t, axis=1, keepdims=True)
    norm = jnp.sum(dot_nn(coef_t, mass) * coef_t, axis=1, keepdims=True)
    rest_t = jnp.where(iota((MODES, WIDE), 1) >= MODES, coef_t, 0.0)
    top = dot_nn(dot_nn(rest_t, cross), corner[:, MODES:2 * MODES])
    search_t = rest_t - jnp.concatenate([top, jnp.zeros((MODES, WIDE - MODES), F32)], axis=1)
    return coef_t, search_t, ritz, ritz / norm


def kernel(ngx, ngy, x_ref, p_ref, s_ref, d_ref, xo_ref, po_ref, rz_ref,
           ext, w2, q, k0, pk, side, th_x, th_y, gr_x, gr_y,
           h_send, h_recv, th_xs, th_xr, th_ys, th_yr, gr_xs, gr_xr, gr_ys, gr_yr):
    rows, lanes = s_ref.shape
    full = lanes + 128
    gx, gy = lax.axis_index("gx"), lax.axis_index("gy")
    lane_id = iota((1, full), 1)
    depth = lane_id % NZ
    low = (depth >= 1).astype(F32)
    high = (depth <= NZ - 2).astype(F32)
    tile_id = iota((1, 128), 1)

    barrier = pltpu.get_barrier_semaphore()
    for o in range(1, ngx):
        pl.semaphore_signal(barrier, inc=1, device_id=(lax.rem(gx + o, ngx), gy), device_id_type=MESH)
    for o in range(1, ngy):
        pl.semaphore_signal(barrier, inc=1, device_id=(gx, lax.rem(gy + o, ngy)), device_id_type=MESH)

    def exists(dx, dy):
        good = None
        for cond in ([gx > 0] if dx < 0 else [gx < ngx - 1] if dx > 0 else []) + (
                [gy > 0] if dy < 0 else [gy < ngy - 1] if dy > 0 else []):
            good = cond if good is None else jnp.logical_and(good, cond)
        return good

    for dx in (1, ngx - 1):
        for dy in (1, ngy - 1):
            pl.semaphore_signal(barrier, inc=1, device_id_type=MESH,
                                device_id=(lax.rem(gx + dx, ngx), lax.rem(gy + dy, ngy)))
    pl.semaphore_wait(barrier, ngx - 1 + ngy - 1 + 4)

    for r in range(rows):
        ext[r + 1, XLO:PLO, 0:lanes] = x_ref[:, r, :]
        ext[r + 1, PLO:RLO, 0:lanes] = p_ref[:, r, :]
        ext[r + 1, COEF:COEF + 8, 0:lanes] = jnp.concatenate(
            [s_ref[r:r + 1, :], jnp.sqrt(d_ref[r:r + 1, :]), jnp.zeros((6, lanes), F32)], axis=0)
        q[r, 2 * WIDE:2 * WIDE + MODES, :] = x_ref[:, r, :]

    steps = [(dx, dy) for dx in (-1, 0, 1) for dy in (-1, 0, 1) if (dx, dy) != (0, 0)]

    def exchange(phase, lo, hi):
        left = jnp.zeros((hi - lo, 128), F32)
        right = jnp.zeros((hi - lo, 128), F32)
        for r in range(rows):
            here = jnp.logical_and(tile_id >= NZ * r, tile_id < NZ * (r + 1))
            first = ext[r + 1, lo:hi, 0:128]
            last = pltpu.roll(ext[r + 1, lo:hi, lanes - 128:lanes], NZ, 1)
            if r:
                first, last = pltpu.roll(first, NZ * r, 1), pltpu.roll(last, NZ * r, 1)
            left, right = jnp.where(here, first, left), jnp.where(here, last, right)
        pk[0, lo:hi, :] = left
        pk[1, lo:hi, :] = right
        copies = []
        for i, (dx, dy) in enumerate(steps):
            back = steps.index((-dx, -dy))
            if dy == 0:
                src = ext.at[1 if dx < 0 else rows, lo:hi, 0:lanes]
                dst = ext.at[rows + 1 if dx < 0 else 0, lo:hi, 0:lanes]
            else:
                src = pk.at[0 if dy < 0 else 1, lo:hi]
                dst = side.at[back, lo:hi]
            copy = pltpu.make_async_remote_copy(
                src_ref=src, dst_ref=dst, send_sem=h_send.at[phase, i], recv_sem=h_recv.at[phase, back],
                device_id=(gx + dx, gy + dy), device_id_type=MESH)
            copies.append(copy)
            there = exists(dx, dy)

            @pl.when(there)
            def _(copy=copy):
                copy.start()

            @pl.when(jnp.logical_not(there))
            def _(i=i, dx=dx, dy=dy):
                if dy == 0:
                    ext[0 if dx < 0 else rows + 1, lo:hi, 0:lanes] = jnp.zeros((hi - lo, lanes), F32)
                else:
                    side[i, lo:hi, :] = jnp.zeros((hi - lo, 128), F32)
        for i, (dx, dy) in enumerate(steps):
            back = steps.index((-dx, -dy))

            @pl.when(exists(dx, dy))
            def _(i=i, back=back):
                copies[i].wait_send()
                copies[back].wait_recv()
        for e in range(rows + 2):
            dx, r = (-1, rows - 1) if e == 0 else (1, 0) if e == rows + 1 else (0, e - 1)
            from_left = side[steps.index((dx, -1)), lo:hi, :]
            from_right = side[steps.index((dx, 1)), lo:hi, :]
            from_left = pltpu.roll(from_left, (112 - NZ * r) % 128, 1) if (112 - NZ * r) % 128 else from_left
            from_right = pltpu.roll(from_right, (128 - NZ * r) % 128, 1) if r else from_right
            ext[e, lo:hi, lanes:full] = jnp.where(
                tile_id < NZ, from_right, jnp.where(tile_id >= 128 - NZ, from_left, 0.0))

    def reduce_line(size, me, place, value, slots, send, recv):
        slots[me] = value
        copies = []
        for o in range(1, size):
            copy = pltpu.make_async_remote_copy(
                src_ref=slots.at[me], dst_ref=slots.at[me], send_sem=send.at[o], recv_sem=recv.at[o],
                device_id=place(lax.rem(me + o, size)), device_id_type=MESH)
            copy.start()
            copies.append(copy)
        for copy in copies:
            copy.wait()
        total = slots[0]
        for o in range(1, size):
            total = total + slots[o]
        return total

    def all_reduce(value, sx, sy, xs, xr, ys, yr):
        value = reduce_line(ngx, gx, lambda other: (other, gy), value, sx, xs, xr)
        return reduce_line(ngy, gy, lambda other: (gx, other), value, sy, ys, yr)

    def plane(value, center, edge):
        if center == 1.0:
            value = value + edge * (pltpu.roll(value, 1, 1) * low + pltpu.roll(value, full - 1, 1) * high)
            return value + edge * (pltpu.roll(value, NZ, 1) + pltpu.roll(value, full - NZ, 1))
        value = center * value + (pltpu.roll(value, 1, 1) * low + pltpu.roll(value, full - 1, 1) * high)
        return center * value + (pltpu.roll(value, NZ, 1) + pltpu.roll(value, full - NZ, 1))

    def operators(r, lo):
        before, here, after = [ext[r + j, lo:lo + MODES, :] for j in range(3)]
        s_b, s_h, s_a = [ext[r + j, 0:1, :] for j in range(3)]
        d_b, d_h, d_a = [ext[r + j, 1:2, :] for j in range(3)]
        plain = plane(here + 0.5 * (before + after), 1.0, 0.5)
        stiff = plane(s_h * here + 0.5 * (s_b * before + s_a * after), 1.0, 0.5)
        mass = plane(4.0 * (d_h * here) + (d_b * before + d_a * after), 4.0, 1.0)
        field = here[:, 0:lanes]
        k_out = field * k0[r, 0:1, :] - s_h[:, 0:lanes] * plain[:, 0:lanes] - stiff[:, 0:lanes]
        m_out = (d_h[:, 0:lanes] * (1.0 / 216.0)) * mass[:, 0:lanes]
        return field, k_out, m_out

    exchange(0, COEF, RLO)

    def coef_row(r, carry):
        before, here, after = [ext[r + j, 0:8, :] for j in range(3)]
        near = plane(here + 0.5 * (before + after), 1.0, 0.5)
        k0[r] = 8.0 * here[:, 0:lanes] + near[:, 0:lanes]
        return carry

    lax.fori_loop(0, rows, coef_row, 0)

    def fold(value):
        total = value[:, 0:128]
        for j in range(1, lanes // 128):
            total = total + value[:, 128 * j:128 * (j + 1)]
        return total

    def mode_row(r, carry):
        field, k_out, m_out = operators(r, XLO)
        q[r, 0:MODES, :] = k_out
        q[r, WIDE:WIDE + MODES, :] = m_out
        return carry[0] + fold(field * k_out), carry[1] + fold(field * m_out)

    zero = jnp.zeros((MODES, 128), F32)
    numer, denom = lax.fori_loop(0, rows, mode_row, (zero, zero))
    sums = all_reduce(jnp.concatenate([numer, denom], axis=0), th_x, th_y, th_xs, th_xr, th_ys, th_yr)
    sums = jnp.sum(sums, axis=1, keepdims=True)
    theta = sums[0:MODES] / sums[MODES:2 * MODES]

    def residual_row(r, carry):
        ext[r + 1, RLO:R2LO, 0:lanes] = q[r, 0:MODES, :] - q[r, WIDE:WIDE + MODES, :] * theta
        return carry

    lax.fori_loop(0, rows, residual_row, 0)
    exchange(1, RLO, R2LO)

    def rest_row(r, total):
        _, k_out, m_out = operators(r, PLO)
        q[r, MODES:2 * MODES, :] = k_out
        q[r, WIDE + MODES:WIDE + 2 * MODES, :] = m_out
        _, k_out, m_out = operators(r, RLO)
        q[r, 2 * MODES:WIDE, :] = k_out
        q[r, WIDE + 2 * MODES:2 * WIDE, :] = m_out
        return total + dot_nt(ext[r + 1, XLO:R2LO, 0:lanes], q[r])

    q_pad = q.shape[1] - 2 * WIDE - MODES
    for r in range(rows):
        q[r, 2 * WIDE + MODES:, :] = jnp.zeros((q_pad, lanes), F32)
    table = lax.fori_loop(0, rows, rest_row, jnp.zeros((WIDE, 128), F32))
    table = all_reduce(table, gr_x.at[0], gr_y.at[0], gr_xs.at[0], gr_xr.at[0], gr_ys.at[0], gr_yr.at[0])
    coef_t, search_t, _, theta2 = small_problem(table)
    both = jnp.concatenate([coef_t, search_t], axis=0)

    def move_row(r, carry):
        new = dot_nn(both, ext[r + 1, XLO:R2LO, 0:lanes])
        new_k = dot_nn(both, q[r, 0:WIDE, :])
        new_m = dot_nn(both, q[r, WIDE:2 * WIDE, :])
        res = new_k[0:MODES] - new_m[0:MODES] * theta2
        w2[r, 0:2 * MODES, :] = new
        w2[r, 2 * MODES:WIDE, :] = res
        ext[r + 1, R2LO:TOP, 0:lanes] = res
        q[r, 0:2 * MODES, :] = new_k
        q[r, WIDE:WIDE + 2 * MODES, :] = new_m
        q[r, 2 * WIDE:2 * WIDE + MODES, :] = new[0:MODES]
        return carry

    lax.fori_loop(0, rows, move_row, 0)
    exchange(2, R2LO, TOP)

    def last_row(r, total):
        _, k_out, m_out = operators(r, R2LO)
        q[r, 2 * MODES:WIDE, :] = k_out
        q[r, WIDE + 2 * MODES:2 * WIDE, :] = m_out
        return total + dot_nt(w2[r], q[r])

    table = lax.fori_loop(0, rows, last_row, jnp.zeros((WIDE, 128), F32))
    table = all_reduce(table, gr_x.at[1], gr_y.at[1], gr_xs.at[1], gr_xr.at[1], gr_ys.at[1], gr_yr.at[1])
    coef_t, search_t, ritz, _ = small_problem(table)
    both = jnp.concatenate([coef_t, search_t], axis=0) * math.sqrt(rows * lanes * ngx * ngy)
    for r in range(rows):
        new = dot_nn(both, w2[r])
        xo_ref[:, r, :] = new[0:MODES]
        po_ref[:, r, :] = new[MODES:2 * MODES]
    rz_ref[...] = jnp.sum(
        jnp.where(iota((MODES, 128), 0) == iota((MODES, 128), 1), ritz, 0.0), axis=0, keepdims=True)


def solution(mesh):
    ngx, ngy = mesh.shape["gx"], mesh.shape["gy"]

    def on_device(modes_start, search_start, stiffness, density):
        rows, lanes = stiffness.shape
        dma = pltpu.SemaphoreType.DMA
        modes, search, ritz = pl.pallas_call(
            functools.partial(kernel, ngx, ngy),
            out_shape=(
                jax.ShapeDtypeStruct(modes_start.shape, F32),
                jax.ShapeDtypeStruct(modes_start.shape, F32),
                jax.ShapeDtypeStruct((1, 128), F32),
            ),
            in_specs=[pl.BlockSpec(memory_space=pltpu.VMEM)] * 4,
            out_specs=[pl.BlockSpec(memory_space=pltpu.VMEM)] * 3,
            scratch_shapes=[
                pltpu.VMEM((rows + 2, TOP, lanes + 128), F32),
                pltpu.VMEM((rows, WIDE, lanes), F32),
                pltpu.VMEM((rows, 128, lanes), F32),
                pltpu.VMEM((rows, 8, lanes), F32),
                pltpu.VMEM((2, TOP, 128), F32),
                pltpu.VMEM((8, TOP, 128), F32),
                pltpu.VMEM((ngx, 2 * MODES, 128), F32),
                pltpu.VMEM((ngy, 2 * MODES, 128), F32),
                pltpu.VMEM((2, ngx, WIDE, 128), F32),
                pltpu.VMEM((2, ngy, WIDE, 128), F32),
                dma((3, 8)), dma((3, 8)),
                dma((ngx,)), dma((ngx,)), dma((ngy,)), dma((ngy,)),
                dma((2, ngx)), dma((2, ngx)), dma((2, ngy)), dma((2, ngy)),
            ],
            compiler_params=pltpu.CompilerParams(
                collective_id=0, has_side_effects=True, vmem_limit_bytes=40 * 1024 * 1024),
        )(modes_start, search_start, stiffness, density)
        return modes, search, ritz[0, 0:MODES]

    return jax.shard_map(
        on_device, mesh=mesh,
        in_specs=(P(None, "gx", "gy"), P(None, "gx", "gy"), P("gx", "gy"), P("gx", "gy")),
        out_specs=(P(None, "gx", "gy"), P(None, "gx", "gy"), P()),
        check_vma=False,
    )
```

time: 549 us -> 93.4 us (0.17); the launches traced: 541 us -> 93 us
  other arithmetic: 198 us -> 0 us
  blocking collectives: 169 us -> 0 us
  Pallas kernels: 0 us -> 87.1 us
  starting transfers between devices: 63.8 us -> 0 us
  local copies, waits for them, and re-layouts: 48.4 us -> 5.24 us
  waiting for transfers between devices: 31.8 us -> 0 us
  matrix products: 25.3 us -> 0 us
    psum x4 -> x0, blocking collectives: 169 us -> none  [the longest x2 86.2 us: rayleigh_sums(): lax.psum((jnp.sum(current * stiff_modes, axis=1), jnp.sum(current * mass_...]
    another operation x110 -> x0, other arithmetic: 136 us -> none  [the longest x30 50.5 us: reduce_block(): jnp.linalg.cholesky(jnp.dot(lower_gram, lower_gram.T, precision=lax.Preci...]
    pallas_call x0 -> x1, Pallas kernels: none -> 87.1 us  [on_device(): pl.pallas_call(functools.partial(kernel, ngx, ngy), out_shape=(jax.ShapeD...]
    ppermute x30 -> x0, starting transfers between devices: 63.8 us -> none  [the longest x10 30.4 us: with_halo(): before = lax.ppermute(last, axis, up)]
    ppermute x30 -> x0, waiting for transfers between devices: 31.8 us -> none  [the longest x10 18.6 us: swapped(): lax.ppermute(value, axis, [(i, i ^ 1 << distance) for i in range(lax.axis...]
    reshape x15 -> x0, local copies, waits for them, and re-layouts: 21.3 us -> none  [the longest x8 14.1 us: flatten_padded(): padded.reshape(padded.shape[:-2] + (padded.shape[-2] * padded.shape[-1],))]
    dot_general x67 -> x0, matrix products: 16.8 us -> none  [the longest x12 1.89 us: small_problem(): jnp.dot(proj_mass, solved, precision=lax.Precision.HIGHEST)]
    concatenate x6 -> x0, other arithmetic: 15.8 us -> none  [the longest x5 15 us: with_halo(): value = jnp.concatenate([before, value, after], axis=dim)]
  transfers between devices with their start and end apart: 30 -> 0, of which waited for: 12 -> 0; matrix products, arithmetic and copies ran while one was open for 17% -> 0% of each run, Pallas kernels for 0% -> 0%
where the time goes in v1:
time: 93.4 us; the launch traced here: 93 us
  Pallas kernels  87.1 us (93%)
  local copies, waits for them, and re-layouts  5.24 us (6%)
    pallas_call x1, Pallas kernels, on_device(): pl.pallas_call(functools.partial(kernel, ngx, ngy), out_shape=(jax.ShapeD...  87.1 us
    unnamed x10, local copies, waits for them, and re-layouts  4.73 us

profile of v1, /device:TPU:0, one launch (start us, length us, event | category | flops | bytes accessed | tf_op | source)
XLA Modules:
  0.0 93.0 jit_solution(1961054979142759492)
XLA Ops:
  0.6 0.0 copy-start
  0.6 0.9 %copy-done = f32[16,8,512]{2,1,0:T(8,128)S(1)} copy-done((f32[16,8,512]{2,1,0:T(8,128)S(1)}, f32[16,8,512]{2,1,0:T(8,128)}, u32[]{:S(2)}) %copy-start) | copy-done | bytes 262168
  1.6 0.0 copy-start.1
  1.6 0.9 %copy-done.1 = f32[16,8,512]{2,1,0:T(8,128)S(1)} copy-done((f32[16,8,512]{2,1,0:T(8,128)S(1)}, f32[16,8,512]{2,1,0:T(8,128)}, u32[]{:S(2)}) %copy-start.1) | copy-done | bytes 262168
  2.5 0.0 copy-start.2
  2.5 0.7 copy-done.2
  3.3 0.0 copy-start.3
  3.3 0.7 copy-done.3
  4.0 87.1 %shard_map.67 = (f32[16,8,512]{2,1,0:T(8,128)S(1)}, f32[16,8,512]{2,1,0:T(8,128)S(1)}, f32[1,128]{1,0:T(1,128)S(1)}) custom-call(f32[16,8,512]{2,1,0:T(8,128)S(1)} %copy-done, f32[16,8,512]{2,1,0:T(8,128)S(1)} %copy-done.1, f32[8,512]{1,0:T(8,128)S(1)} %copy-done.2, f32[8,512]{1,0:T(8,128)S(1)} %copy-done.3), custom_call_target="tpu_custom_call" | custom-call | tf_op jit(solution)/shard_map/pallas_call | solution.py:301
  91.1 0.5 slice_bitcast_fusion
  91.6 0.7 copy.9
  92.3 0.7 copy.10
Async XLA Ops:
  0.6 1.0 %copy-start = (f32[16,8,512]{2,1,0:T(8,128)S(1)}, f32[16,8,512]{2,1,0:T(8,128)}, u32[]{:S(2)}) copy-start(f32[16,8,512]{2,1,0:T(8,128)} %x_ref.1) | copy-start | bytes 786436
  1.6 0.9 %copy-start.1 = (f32[16,8,512]{2,1,0:T(8,128)S(1)}, f32[16,8,512]{2,1,0:T(8,128)}, u32[]{:S(2)}) copy-start(f32[16,8,512]{2,1,0:T(8,128)} %p_ref.1) | copy-start | bytes 786436
  2.5 0.7 copy-start.2
  3.3 0.7 copy-start.3

commit v2 on v1

--- a/solution.py
+++ b/solution.py
@@ -32,18 +32,38 @@
     return lax.broadcasted_iota(jnp.int32, shape, dim)
 
 
-def jordan_step(table, k):
-    rows = table.shape[0]
-    pivot_row = table[k:k + 1, :] * (1.0 / table[k:k + 1, k:k + 1])
-    return jnp.where(iota((rows, 1), 0) == k, pivot_row, table - table[:, k:k + 1] * pivot_row)
+def jordan_pair(table, k):
+    row_id = iota((table.shape[0], 1), 0)
+    first, second = table[:, k:k + 1], table[:, k + 1:k + 2]
+    top, low = table[k:k + 1, :], table[k + 1:k + 2, :]
+    corner = top[:, k + 1:k + 2]
+    inverse = 1.0 / top[:, k:k + 1]
+    ratio = low[:, k:k + 1] * inverse
+    low = (low - ratio * top) * (1.0 / (low[:, k + 1:k + 2] - ratio * corner))
+    top = (top - corner * low) * inverse
+    rest = table - first * top - second * low
+    return jnp.where(row_id == k, top, jnp.where(row_id == k + 1, low, rest))
 
 
 def orthonormal(gram, rows_t):
     count = gram.shape[0]
     row_id = iota((count, 1), 0)
-    for k in range(count - 1):
-        factor = jnp.where(row_id > k, gram[:, k:k + 1] * (1.0 / gram[k:k + 1, k:k + 1]), 0.0)
-        gram, rows_t = gram - factor * gram[k:k + 1, :], rows_t - factor * rows_t[k:k + 1, :]
+    for k in range(0, count, 2):
+        first, second = gram[:, k:k + 1], gram[:, k + 1:k + 2]
+        corner = gram[k:k + 1, k + 1:k + 2]
+        inverse = 1.0 / gram[k:k + 1, k:k + 1]
+        ratio = gram[k + 1:k + 2, k:k + 1] * inverse
+        factor = first * inverse
+        other = (second - factor * corner) * (
+            1.0 / (gram[k + 1:k + 2, k + 1:k + 2] - ratio * corner))
+        factor = jnp.where(row_id > k, factor, 0.0)
+        other = jnp.where(row_id > k + 1, other, 0.0)
+
+        def eliminate(value):
+            top = value[k:k + 1, :]
+            return value - factor * top - other * (value[k + 1:k + 2, :] - ratio * top)
+
+        gram, rows_t = eliminate(gram), eliminate(rows_t)
     diag = jnp.sum(jnp.where(iota(gram.shape, 0) == iota(gram.shape, 1), gram, 0.0),
                    axis=1, keepdims=True)
     return rows_t * lax.rsqrt(diag)
@@ -56,10 +76,10 @@
     solved = table
     corner = jnp.concatenate(
         [cross[0:MODES], (iota((MODES, MODES), 0) == iota((MODES, MODES), 1)).astype(F32)], axis=1)
-    for k in range(WIDE):
-        solved = jordan_step(solved, k)
+    for k in range(0, WIDE, 2):
+        solved = jordan_pair(solved, k)
         if k < MODES:
-            corner = jordan_step(corner, k)
+            corner = jordan_pair(corner, k)
     step = solved[:, WIDE:2 * WIDE]
     coef_t = (iota((MODES, WIDE), 0) == iota((MODES, WIDE), 1)).astype(F32)
     for power in POWERS:
@@ -74,9 +94,10 @@
     return coef_t, search_t, ritz, ritz / norm
 
 
-def kernel(ngx, ngy, x_ref, p_ref, s_ref, d_ref, xo_ref, po_ref, rz_ref,
-           ext, w2, q, k0, pk, side, th_x, th_y, gr_x, gr_y,
-           h_send, h_recv, th_xs, th_xr, th_ys, th_yr, gr_xs, gr_xr, gr_ys, gr_yr):
+def kernel(ngx, ngy, x_hbm, p_hbm, s_hbm, d_hbm, xo_ref, po_ref, rz_ref,
+           x_ref, p_ref, s_ref, d_ref, ext, w2, q, kx, k0, pk, side, th_x, th_y, sc_src, sc_dst, gr_y, gat,
+           in_sem, h_send, h_recv, th_xs, th_xr, th_ys, th_yr,
+           rs_s, rs_r, gr_ys, gr_yr, ag_s, ag_r):
     rows, lanes = s_ref.shape
     full = lanes + 128
     gx, gy = lax.axis_index("gx"), lax.axis_index("gy")
@@ -85,6 +106,10 @@
     low = (depth >= 1).astype(F32)
     high = (depth <= NZ - 2).astype(F32)
     tile_id = iota((1, 128), 1)
+    inputs = [pltpu.make_async_copy(src, dst, in_sem.at[i]) for i, (src, dst) in enumerate(
+        ((s_hbm, s_ref), (d_hbm, d_ref), (x_hbm, x_ref), (p_hbm, p_ref)))]
+    for copy in inputs:
+        copy.start()
 
     barrier = pltpu.get_barrier_semaphore()
     for o in range(1, ngx):
@@ -105,16 +130,21 @@
                                 device_id=(lax.rem(gx + dx, ngx), lax.rem(gy + dy, ngy)))
     pl.semaphore_wait(barrier, ngx - 1 + ngy - 1 + 4)
 
+    for copy in inputs:
+        copy.wait()
+    q_pad = q.shape[1] - 2 * WIDE - MODES
     for r in range(rows):
-        ext[r + 1, XLO:PLO, 0:lanes] = x_ref[:, r, :]
+        modes_row = x_ref[:, r, :]
+        ext[r + 1, XLO:PLO, 0:lanes] = modes_row
         ext[r + 1, PLO:RLO, 0:lanes] = p_ref[:, r, :]
         ext[r + 1, COEF:COEF + 8, 0:lanes] = jnp.concatenate(
             [s_ref[r:r + 1, :], jnp.sqrt(d_ref[r:r + 1, :]), jnp.zeros((6, lanes), F32)], axis=0)
-        q[r, 2 * WIDE:2 * WIDE + MODES, :] = x_ref[:, r, :]
+        q[r, 2 * WIDE:2 * WIDE + MODES, :] = modes_row
+        q[r, 2 * WIDE + MODES:, :] = jnp.zeros((q_pad, lanes), F32)
 
     steps = [(dx, dy) for dx in (-1, 0, 1) for dy in (-1, 0, 1) if (dx, dy) != (0, 0)]
 
-    def exchange(phase, lo, hi):
+    def send_rims(phase, lo, hi):
         left = jnp.zeros((hi - lo, 128), F32)
         right = jnp.zeros((hi - lo, 128), F32)
         for r in range(rows):
@@ -151,6 +181,9 @@
                     ext[0 if dx < 0 else rows + 1, lo:hi, 0:lanes] = jnp.zeros((hi - lo, lanes), F32)
                 else:
                     side[i, lo:hi, :] = jnp.zeros((hi - lo, 128), F32)
+        return copies
+
+    def take_rims(copies, lo, hi):
         for i, (dx, dy) in enumerate(steps):
             back = steps.index((-dx, -dy))
 
@@ -167,25 +200,53 @@
             ext[e, lo:hi, lanes:full] = jnp.where(
                 tile_id < NZ, from_right, jnp.where(tile_id >= 128 - NZ, from_left, 0.0))
 
-    def reduce_line(size, me, place, value, slots, send, recv):
-        slots[me] = value
+    def swap_line(size, me, place, source, slots, send, recv):
         copies = []
         for o in range(1, size):
+            to = lax.rem(me + o, size)
             copy = pltpu.make_async_remote_copy(
-                src_ref=slots.at[me], dst_ref=slots.at[me], send_sem=send.at[o], recv_sem=recv.at[o],
-                device_id=place(lax.rem(me + o, size)), device_id_type=MESH)
+                src_ref=source(to), dst_ref=slots.at[me], send_sem=send.at[o], recv_sem=recv.at[o],
+                device_id=place(to), device_id_type=MESH)
             copy.start()
             copies.append(copy)
         for copy in copies:
             copy.wait()
-        total = slots[0]
-        for o in range(1, size):
-            total = total + slots[o]
-        return total
-
-    def all_reduce(value, sx, sy, xs, xr, ys, yr):
-        value = reduce_line(ngx, gx, lambda other: (other, gy), value, sx, xs, xr)
-        return reduce_line(ngy, gy, lambda other: (gx, other), value, sy, ys, yr)
+
+    def add_up(slots, size):
+        parts = [slots[o] for o in range(size)]
+        while len(parts) > 1:
+            parts = [a + b for a, b in zip(parts[::2], parts[1::2])] + parts[len(parts) // 2 * 2:]
+        return parts[0]
+
+    def in_column(other):
+        return other, gy
+
+    def in_row(other):
+        return gx, other
+
+    def line_sum(size, me, place, value, slots, send, recv):
+        slots[me] = value
+        swap_line(size, me, place, lambda to: slots.at[me], slots, send, recv)
+        return add_up(slots, size)
+
+    def table_sum(it, table):
+        block = -(-WIDE // ngx)
+        tall = sc_src.shape[2]
+        for o in range(ngx):
+            piece = table[min(WIDE, block * o):min(WIDE, block * (o + 1))]
+            short = tall - piece.shape[0]
+            if short == tall:
+                piece = jnp.zeros((tall, 128), F32)
+            elif short:
+                piece = jnp.concatenate([piece, jnp.zeros((short, 128), F32)], axis=0)
+            sc_src[it, o] = piece
+        sc_dst[it, gx] = sc_src[it, gx]
+        swap_line(ngx, gx, in_column, lambda to: sc_src.at[it, to], sc_dst.at[it], rs_s.at[it], rs_r.at[it])
+        part = add_up(sc_dst.at[it], ngx)
+        part = line_sum(ngy, gy, in_row, part, gr_y.at[it], gr_ys.at[it], gr_yr.at[it])
+        gat[it, gx] = part
+        swap_line(ngx, gx, in_column, lambda to: gat.at[it, gx], gat.at[it], ag_s.at[it], ag_r.at[it])
+        return jnp.concatenate([gat[it, o, 0:block] for o in range(-(-WIDE // block))], axis=0)[0:WIDE]
 
     def plane(value, center, edge):
         if center == 1.0:
@@ -206,7 +267,9 @@
         m_out = (d_h[:, 0:lanes] * (1.0 / 216.0)) * mass[:, 0:lanes]
         return field, k_out, m_out
 
-    exchange(0, COEF, RLO)
+    rims = send_rims(0, COEF, PLO)
+    search_rims = send_rims(1, PLO, RLO)
+    take_rims(rims, COEF, PLO)
 
     def coef_row(r, carry):
         before, here, after = [ext[r + j, 0:8, :] for j in range(3)]
@@ -230,8 +293,12 @@
 
     zero = jnp.zeros((MODES, 128), F32)
     numer, denom = lax.fori_loop(0, rows, mode_row, (zero, zero))
-    sums = all_reduce(jnp.concatenate([numer, denom], axis=0), th_x, th_y, th_xs, th_xr, th_ys, th_yr)
-    sums = jnp.sum(sums, axis=1, keepdims=True)
+    pair = iota((2 * MODES, 128), 0) == iota((2 * MODES, 128), 1)
+    sums = jnp.sum(jnp.concatenate([numer, denom], axis=0), axis=1, keepdims=True)
+    sums = jnp.broadcast_to(jnp.sum(jnp.where(pair, sums, 0.0), axis=0, keepdims=True), (8, 128))
+    sums = line_sum(ngx, gx, in_column, sums, th_x, th_xs, th_xr)
+    sums = line_sum(ngy, gy, in_row, sums, th_y, th_ys, th_yr)
+    sums = jnp.sum(jnp.where(pair, sums[0:1], 0.0), axis=1, keepdims=True)
     theta = sums[0:MODES] / sums[MODES:2 * MODES]
 
     def residual_row(r, carry):
@@ -239,40 +306,55 @@
         return carry
 
     lax.fori_loop(0, rows, residual_row, 0)
-    exchange(1, RLO, R2LO)
-
-    def rest_row(r, total):
+    rims = send_rims(2, RLO, R2LO)
+    take_rims(search_rims, PLO, RLO)
+
+    def search_row(r, carry):
         _, k_out, m_out = operators(r, PLO)
         q[r, MODES:2 * MODES, :] = k_out
         q[r, WIDE + MODES:WIDE + 2 * MODES, :] = m_out
+        return carry
+
+    lax.fori_loop(0, rows, search_row, 0)
+    take_rims(rims, RLO, R2LO)
+
+    def rest_row(r, total):
         _, k_out, m_out = operators(r, RLO)
         q[r, 2 * MODES:WIDE, :] = k_out
         q[r, WIDE + 2 * MODES:2 * WIDE, :] = m_out
         return total + dot_nt(ext[r + 1, XLO:R2LO, 0:lanes], q[r])
 
-    q_pad = q.shape[1] - 2 * WIDE - MODES
-    for r in range(rows):
-        q[r, 2 * WIDE + MODES:, :] = jnp.zeros((q_pad, lanes), F32)
-    table = lax.fori_loop(0, rows, rest_row, jnp.zeros((WIDE, 128), F32))
-    table = all_reduce(table, gr_x.at[0], gr_y.at[0], gr_xs.at[0], gr_xr.at[0], gr_ys.at[0], gr_yr.at[0])
+    table = table_sum(0, lax.fori_loop(0, rows, rest_row, jnp.zeros((WIDE, 128), F32)))
     coef_t, search_t, _, theta2 = small_problem(table)
     both = jnp.concatenate([coef_t, search_t], axis=0)
 
+    def next_residual_row(r, carry):
+        new_k = dot_nn(coef_t, q[r, 0:WIDE, :])
+        new_m = dot_nn(coef_t, q[r, WIDE:2 * WIDE, :])
+        res = new_k - new_m * theta2
+        kx[r, 0:MODES, :] = new_k
+        kx[r, MODES:2 * MODES, :] = new_m
+        w2[r, 2 * MODES:WIDE, :] = res
+        ext[r + 1, R2LO:TOP, 0:lanes] = res
+        return carry
+
+    lax.fori_loop(0, rows, next_residual_row, 0)
+    rims = send_rims(3, R2LO, TOP)
+
     def move_row(r, carry):
         new = dot_nn(both, ext[r + 1, XLO:R2LO, 0:lanes])
-        new_k = dot_nn(both, q[r, 0:WIDE, :])
-        new_m = dot_nn(both, q[r, WIDE:2 * WIDE, :])
-        res = new_k[0:MODES] - new_m[0:MODES] * theta2
+        new_k = dot_nn(search_t, q[r, 0:WIDE, :])
+        new_m = dot_nn(search_t, q[r, WIDE:2 * WIDE, :])
         w2[r, 0:2 * MODES, :] = new
-        w2[r, 2 * MODES:WIDE, :] = res
-        ext[r + 1, R2LO:TOP, 0:lanes] = res
-        q[r, 0:2 * MODES, :] = new_k
-        q[r, WIDE:WIDE + 2 * MODES, :] = new_m
+        q[r, 0:MODES, :] = kx[r, 0:MODES, :]
+        q[r, MODES:2 * MODES, :] = new_k
+        q[r, WIDE:WIDE + MODES, :] = kx[r, MODES:2 * MODES, :]
+        q[r, WIDE + MODES:WIDE + 2 * MODES, :] = new_m
         q[r, 2 * WIDE:2 * WIDE + MODES, :] = new[0:MODES]
         return carry
 
     lax.fori_loop(0, rows, move_row, 0)
-    exchange(2, R2LO, TOP)
+    take_rims(rims, R2LO, TOP)
 
     def last_row(r, total):
         _, k_out, m_out = operators(r, R2LO)
@@ -280,8 +362,7 @@
         q[r, WIDE + 2 * MODES:2 * WIDE, :] = m_out
         return total + dot_nt(w2[r], q[r])
 
-    table = lax.fori_loop(0, rows, last_row, jnp.zeros((WIDE, 128), F32))
-    table = all_reduce(table, gr_x.at[1], gr_y.at[1], gr_xs.at[1], gr_xr.at[1], gr_ys.at[1], gr_yr.at[1])
+    table = table_sum(1, lax.fori_loop(0, rows, last_row, jnp.zeros((WIDE, 128), F32)))
     coef_t, search_t, ritz, _ = small_problem(table)
     both = jnp.concatenate([coef_t, search_t], axis=0) * math.sqrt(rows * lanes * ngx * ngy)
     for r in range(rows):
@@ -298,6 +379,7 @@
     def on_device(modes_start, search_start, stiffness, density):
         rows, lanes = stiffness.shape
         dma = pltpu.SemaphoreType.DMA
+        tall = -(-(-(-WIDE // ngx)) // 8) * 8
         modes, search, ritz = pl.pallas_call(
             functools.partial(kernel, ngx, ngy),
             out_shape=(
@@ -305,22 +387,29 @@
                 jax.ShapeDtypeStruct(modes_start.shape, F32),
                 jax.ShapeDtypeStruct((1, 128), F32),
             ),
-            in_specs=[pl.BlockSpec(memory_space=pltpu.VMEM)] * 4,
+            in_specs=[pl.BlockSpec(memory_space=pl.ANY)] * 4,
             out_specs=[pl.BlockSpec(memory_space=pltpu.VMEM)] * 3,
             scratch_shapes=[
+                pltpu.VMEM(modes_start.shape, F32),
+                pltpu.VMEM(modes_start.shape, F32),
+                pltpu.VMEM((rows, lanes), F32),
+                pltpu.VMEM((rows, lanes), F32),
                 pltpu.VMEM((rows + 2, TOP, lanes + 128), F32),
                 pltpu.VMEM((rows, WIDE, lanes), F32),
                 pltpu.VMEM((rows, 128, lanes), F32),
+                pltpu.VMEM((rows, 2 * MODES, lanes), F32),
                 pltpu.VMEM((rows, 8, lanes), F32),
                 pltpu.VMEM((2, TOP, 128), F32),
                 pltpu.VMEM((8, TOP, 128), F32),
-                pltpu.VMEM((ngx, 2 * MODES, 128), F32),
-                pltpu.VMEM((ngy, 2 * MODES, 128), F32),
-                pltpu.VMEM((2, ngx, WIDE, 128), F32),
-                pltpu.VMEM((2, ngy, WIDE, 128), F32),
-                dma((3, 8)), dma((3, 8)),
+                pltpu.VMEM((ngx, 8, 128), F32),
+                pltpu.VMEM((ngy, 8, 128), F32),
+                pltpu.VMEM((2, ngx, tall, 128), F32),
+                pltpu.VMEM((2, ngx, tall, 128), F32),
+                pltpu.VMEM((2, ngy, tall, 128), F32),
+                pltpu.VMEM((2, ngx, tall, 128), F32),
+                dma((4,)), dma((4, 8)), dma((4, 8)),
                 dma((ngx,)), dma((ngx,)), dma((ngy,)), dma((ngy,)),
-                dma((2, ngx)), dma((2, ngx)), dma((2, ngy)), dma((2, ngy)),
+                dma((2, ngx)), dma((2, ngx)), dma((2, ngy)), dma((2, ngy)), dma((2, ngx)), dma((2, ngx)),
             ],
             compiler_params=pltpu.CompilerParams(
                 collective_id=0, has_side_effects=True, vmem_limit_bytes=40 * 1024 * 1024),

time: 93.4 us -> 100 us (1.071)
  Pallas kernels: 87.1 us -> 93.7 us
    pallas_call x1, Pallas kernels: 87.1 us -> 93.7 us  [on_device(): pl.pallas_call(functools.partial(kernel, ngx, ngy), out_shape=(jax.ShapeD...]
where the time goes in v2:
time: 100 us; the launch traced here: 99.6 us
  Pallas kernels  93.7 us (94%)
  local copies, waits for them, and re-layouts  5.24 us (5%)
    pallas_call x1, Pallas kernels, on_device(): pl.pallas_call(functools.partial(kernel, ngx, ngy), out_shape=(jax.ShapeD...  93.7 us
    unnamed x10, local copies, waits for them, and re-layouts  4.73 us

profile of v2, /device:TPU:0, one launch (start us, length us, event | category | flops | bytes accessed | tf_op | source)
XLA Modules:
  0.0 99.6 jit_solution(11245261992540640352)
XLA Ops:
  0.6 0.0 copy-start
  0.6 0.9 copy-done
  1.6 0.0 copy-start.1
  1.6 0.9 copy-done.1
  2.5 0.0 copy-start.2
  2.5 0.7 copy-done.2
  3.3 0.0 copy-start.3
  3.3 0.7 copy-done.3
  4.0 93.7 %shard_map.67 = (f32[16,8,512]{2,1,0:T(8,128)S(1)}, f32[16,8,512]{2,1,0:T(8,128)S(1)}, f32[1,128]{1,0:T(1,128)S(1)}) custom-call(f32[16,8,512]{2,1,0:T(8,128)S(1)} %copy-done, f32[16,8,512]{2,1,0:T(8,128)S(1)} %copy-done.1, f32[8,512]{1,0:T(8,128)S(1)} %copy-done.2, f32[8,512]{1,0:T(8,128)S(1)} %copy-done.3), custom_call_target="tpu_custom_call" | custom-call | tf_op jit(solution)/shard_map/pallas_call | solution.py:383
  97.7 0.5 slice_bitcast_fusion
  98.2 0.7 copy.9
  98.9 0.7 copy.10
Async XLA Ops:
  0.6 1.0 copy-start
  1.6 0.9 copy-start.1
  2.5 0.7 copy-start.2
  3.3 0.7 copy-start.3

commit v3 on v2

--- a/solution.py
+++ b/solution.py
@@ -32,38 +32,18 @@
     return lax.broadcasted_iota(jnp.int32, shape, dim)
 
 
-def jordan_pair(table, k):
-    row_id = iota((table.shape[0], 1), 0)
-    first, second = table[:, k:k + 1], table[:, k + 1:k + 2]
-    top, low = table[k:k + 1, :], table[k + 1:k + 2, :]
-    corner = top[:, k + 1:k + 2]
-    inverse = 1.0 / top[:, k:k + 1]
-    ratio = low[:, k:k + 1] * inverse
-    low = (low - ratio * top) * (1.0 / (low[:, k + 1:k + 2] - ratio * corner))
-    top = (top - corner * low) * inverse
-    rest = table - first * top - second * low
-    return jnp.where(row_id == k, top, jnp.where(row_id == k + 1, low, rest))
+def jordan_step(table, k):
+    rows = table.shape[0]
+    pivot_row = table[k:k + 1, :] * (1.0 / table[k:k + 1, k:k + 1])
+    return jnp.where(iota((rows, 1), 0) == k, pivot_row, table - table[:, k:k + 1] * pivot_row)
 
 
 def orthonormal(gram, rows_t):
     count = gram.shape[0]
     row_id = iota((count, 1), 0)
-    for k in range(0, count, 2):
-        first, second = gram[:, k:k + 1], gram[:, k + 1:k + 2]
-        corner = gram[k:k + 1, k + 1:k + 2]
-        inverse = 1.0 / gram[k:k + 1, k:k + 1]
-        ratio = gram[k + 1:k + 2, k:k + 1] * inverse
-        factor = first * inverse
-        other = (second - factor * corner) * (
-            1.0 / (gram[k + 1:k + 2, k + 1:k + 2] - ratio * corner))
-        factor = jnp.where(row_id > k, factor, 0.0)
-        other = jnp.where(row_id > k + 1, other, 0.0)
-
-        def eliminate(value):
-            top = value[k:k + 1, :]
-            return value - factor * top - other * (value[k + 1:k + 2, :] - ratio * top)
-
-        gram, rows_t = eliminate(gram), eliminate(rows_t)
+    for k in range(count - 1):
+        factor = jnp.where(row_id > k, gram[:, k:k + 1] * (1.0 / gram[k:k + 1, k:k + 1]), 0.0)
+        gram, rows_t = gram - factor * gram[k:k + 1, :], rows_t - factor * rows_t[k:k + 1, :]
     diag = jnp.sum(jnp.where(iota(gram.shape, 0) == iota(gram.shape, 1), gram, 0.0),
                    axis=1, keepdims=True)
     return rows_t * lax.rsqrt(diag)
@@ -76,10 +56,10 @@
     solved = table
     corner = jnp.concatenate(
         [cross[0:MODES], (iota((MODES, MODES), 0) == iota((MODES, MODES), 1)).astype(F32)], axis=1)
-    for k in range(0, WIDE, 2):
-        solved = jordan_pair(solved, k)
+    for k in range(WIDE):
+        solved = jordan_step(solved, k)
         if k < MODES:
-            corner = jordan_pair(corner, k)
+            corner = jordan_step(corner, k)
     step = solved[:, WIDE:2 * WIDE]
     coef_t = (iota((MODES, WIDE), 0) == iota((MODES, WIDE), 1)).astype(F32)
     for power in POWERS:
@@ -95,9 +75,9 @@
 
 
 def kernel(ngx, ngy, x_hbm, p_hbm, s_hbm, d_hbm, xo_ref, po_ref, rz_ref,
-           x_ref, p_ref, s_ref, d_ref, ext, w2, q, kx, k0, pk, side, th_x, th_y, sc_src, sc_dst, gr_y, gat,
+           x_ref, p_ref, s_ref, d_ref, ext, w2, q, kx, k0, pk, side, th_x, th_y, gr_x, gr_y,
            in_sem, h_send, h_recv, th_xs, th_xr, th_ys, th_yr,
-           rs_s, rs_r, gr_ys, gr_yr, ag_s, ag_r):
+           gr_xs, gr_xr, gr_ys, gr_yr):
     rows, lanes = s_ref.shape
     full = lanes + 128
     gx, gy = lax.axis_index("gx"), lax.axis_index("gy")
@@ -230,23 +210,8 @@
         return add_up(slots, size)
 
     def table_sum(it, table):
-        block = -(-WIDE // ngx)
-        tall = sc_src.shape[2]
-        for o in range(ngx):
-            piece = table[min(WIDE, block * o):min(WIDE, block * (o + 1))]
-            short = tall - piece.shape[0]
-            if short == tall:
-                piece = jnp.zeros((tall, 128), F32)
-            elif short:
-                piece = jnp.concatenate([piece, jnp.zeros((short, 128), F32)], axis=0)
-            sc_src[it, o] = piece
-        sc_dst[it, gx] = sc_src[it, gx]
-        swap_line(ngx, gx, in_column, lambda to: sc_src.at[it, to], sc_dst.at[it], rs_s.at[it], rs_r.at[it])
-        part = add_up(sc_dst.at[it], ngx)
-        part = line_sum(ngy, gy, in_row, part, gr_y.at[it], gr_ys.at[it], gr_yr.at[it])
-        gat[it, gx] = part
-        swap_line(ngx, gx, in_column, lambda to: gat.at[it, gx], gat.at[it], ag_s.at[it], ag_r.at[it])
-        return jnp.concatenate([gat[it, o, 0:block] for o in range(-(-WIDE // block))], axis=0)[0:WIDE]
+        table = line_sum(ngx, gx, in_column, table, gr_x.at[it], gr_xs.at[it], gr_xr.at[it])
+        return line_sum(ngy, gy, in_row, table, gr_y.at[it], gr_ys.at[it], gr_yr.at[it])
 
     def plane(value, center, edge):
         if center == 1.0:
@@ -379,7 +344,6 @@
     def on_device(modes_start, search_start, stiffness, density):
         rows, lanes = stiffness.shape
         dma = pltpu.SemaphoreType.DMA
-        tall = -(-(-(-WIDE // ngx)) // 8) * 8
         modes, search, ritz = pl.pallas_call(
             functools.partial(kernel, ngx, ngy),
             out_shape=(
@@ -403,13 +367,11 @@
                 pltpu.VMEM((8, TOP, 128), F32),
                 pltpu.VMEM((ngx, 8, 128), F32),
                 pltpu.VMEM((ngy, 8, 128), F32),
-                pltpu.VMEM((2, ngx, tall, 128), F32),
-                pltpu.VMEM((2, ngx, tall, 128), F32),
-                pltpu.VMEM((2, ngy, tall, 128), F32),
-                pltpu.VMEM((2, ngx, tall, 128), F32),
+                pltpu.VMEM((2, ngx, WIDE, 128), F32),
+                pltpu.VMEM((2, ngy, WIDE, 128), F32),
                 dma((4,)), dma((4, 8)), dma((4, 8)),
                 dma((ngx,)), dma((ngx,)), dma((ngy,)), dma((ngy,)),
-                dma((2, ngx)), dma((2, ngx)), dma((2, ngy)), dma((2, ngy)), dma((2, ngx)), dma((2, ngx)),
+                dma((2, ngx)), dma((2, ngx)), dma((2, ngy)), dma((2, ngy)),
             ],
             compiler_params=pltpu.CompilerParams(
                 collective_id=0, has_side_effects=True, vmem_limit_bytes=40 * 1024 * 1024),

time: 100 us -> 90.5 us (0.905)
  Pallas kernels: 93.7 us -> 84.3 us
    pallas_call x1, Pallas kernels: 93.7 us -> 84.3 us  [on_device(): pl.pallas_call(functools.partial(kernel, ngx, ngy), out_shape=(jax.ShapeD...]
where the time goes in v3:
time: 90.5 us; the launch traced here: 90.2 us
  Pallas kernels  84.3 us (93%)
  local copies, waits for them, and re-layouts  5.24 us (6%)
    pallas_call x1, Pallas kernels, on_device(): pl.pallas_call(functools.partial(kernel, ngx, ngy), out_shape=(jax.ShapeD...  84.3 us
    unnamed x10, local copies, waits for them, and re-layouts  4.73 us

profile of v3, /device:TPU:0, one launch (start us, length us, event | category | flops | bytes accessed | tf_op | source)
XLA Modules:
  0.0 90.2 jit_solution(11353922628410709616)
XLA Ops:
  0.6 0.0 copy-start
  0.6 0.9 %copy-done = f32[16,8,512]{2,1,0:T(8,128)S(1)} copy-done((f32[16,8,512]{2,1,0:T(8,128)S(1)}, f32[16,8,512]{2,1,0:T(8,128)}, u32[]{:S(2)}) %copy-start) | copy-done | bytes 262168
  1.6 0.0 copy-start.1
  1.6 0.9 %copy-done.1 = f32[16,8,512]{2,1,0:T(8,128)S(1)} copy-done((f32[16,8,512]{2,1,0:T(8,128)S(1)}, f32[16,8,512]{2,1,0:T(8,128)}, u32[]{:S(2)}) %copy-start.1) | copy-done | bytes 262168
  2.5 0.0 copy-start.2
  2.5 0.7 copy-done.2
  3.3 0.0 copy-start.3
  3.3 0.7 copy-done.3
  4.0 84.3 %shard_map.67 = (f32[16,8,512]{2,1,0:T(8,128)S(1)}, f32[16,8,512]{2,1,0:T(8,128)S(1)}, f32[1,128]{1,0:T(1,128)S(1)}) custom-call(f32[16,8,512]{2,1,0:T(8,128)S(1)} %copy-done, f32[16,8,512]{2,1,0:T(8,128)S(1)} %copy-done.1, f32[8,512]{1,0:T(8,128)S(1)} %copy-done.2, f32[8,512]{1,0:T(8,128)S(1)} %copy-done.3), custom_call_target="tpu_custom_call" | custom-call | tf_op jit(solution)/shard_map/pallas_call | solution.py:347
  88.2 0.5 slice_bitcast_fusion
  88.8 0.7 copy.9
  89.5 0.7 copy.10
Async XLA Ops:
  0.6 1.0 %copy-start = (f32[16,8,512]{2,1,0:T(8,128)S(1)}, f32[16,8,512]{2,1,0:T(8,128)}, u32[]{:S(2)}) copy-start(f32[16,8,512]{2,1,0:T(8,128)} %x_hbm.1) | copy-start | bytes 786436
  1.6 0.9 %copy-start.1 = (f32[16,8,512]{2,1,0:T(8,128)S(1)}, f32[16,8,512]{2,1,0:T(8,128)}, u32[]{:S(2)}) copy-start(f32[16,8,512]{2,1,0:T(8,128)} %p_hbm.1) | copy-start | bytes 786436
  2.5 0.7 copy-start.2
  3.3 0.7 copy-start.3
